TPU v7x, 32 devices: a whole 2x2x4 slice. The times are simulated.
32 devices in a mesh: region: 8 (over z, x), basis: 4 (over y, core).
Axes of the slice: x: 2, y: 2, z: 4, core: 2. Of those that a mesh axis runs over, the one named last changes fastest.
Arguments:
- observations: bfloat16 [262144, 128], P(('region', 'basis')), may hold values from -3 to 4
- basis_values: bfloat16 [262144, 1024], P(('region', 'basis')), as said below
- mixing: bfloat16 [1024, 1024], P('basis'), may hold values from -0.1875 to 0.1875
- pattern: int32 [8, 8], replicated, may hold values 0 or 1
- decays: float32 [8, 1024], P('region', 'basis'), may hold values from 0 to 1
- loadings: float32 [1024], P('basis'), may hold values from 0.3 to 3
Outputs:
- obs_grad: bfloat16 [262144, 128], P(('region', 'basis'))
- attenuation_slope: float32 [8, 1024], P('region', 'basis')
Inputs may be any that keep to these rules, and one draw needn't show every extreme that they name: `basis_values`: every entry lies within 3.5 / 32768 ** 0.5 of zero.
All inputs are finite; a program needn't handle non-finite values.
Results may differ from a plain program's by a relative error of at most 0.015.
Values may be sent and summed in bfloat16 or wider, within the bound.
A program may use at most 128 MiB of HBM per device.

v0:
```python
import jax
import jax.numpy as jnp
from jax import lax
from jax.sharding import PartitionSpec as P

BLOCK = 128


def entering(value, axis, join, neutral, backward):
    count, mine = (lax.axis_size(axis), lax.axis_index(axis))
    pieces = jax.tree.map(lambda part: lax.all_gather(part, axis), value)
    if backward:
        pieces = jax.tree.map(lambda part: part[::-1], pieces)
        mine = count - 1 - mine
    subtotal = jax.tree.map(
        lambda part, zero: jnp.full_like(part, 0) + jnp.asarray(zero, part.dtype), value, neutral
    )

    def turn(position, subtotal):
        longer = join(subtotal, jax.tree.map(lambda part: part[position], pieces))
        return jax.tree.map(lambda new, old: jnp.where(position < mine, new, old), longer, subtotal)

    return lax.fori_loop(0, count - 1, turn, subtotal)


def contract_rows(first_operand, second_operand):
    return lax.dot_general(
        first_operand, second_operand, (((0,), (0,)), ((), ())), preferred_element_type=jnp.float32
    )


def block_rows(mixing, pattern, owner):
    row_count = mixing.shape[0]
    width = mixing.shape[1]
    row_ids = owner * row_count + jnp.arange(row_count)
    column_index = jnp.arange(width)
    labels = jnp.arange(pattern.shape[0])
    row_hot = ((row_ids // BLOCK)[:, None] == labels[None, :]).astype(jnp.float32)
    column_hot = ((column_index // BLOCK)[:, None] == labels[None, :]).astype(jnp.float32)
    expanded = jnp.dot(jnp.dot(row_hot, pattern.astype(jnp.float32)), column_hot.T)
    identity = (row_ids[:, None] == column_index[None, :]).astype(jnp.float32)
    return (identity + mixing.astype(jnp.float32) * expanded).astype(jnp.bfloat16)


def combine(earlier, later):
    return (earlier[0] * later[0], later[0][:, None] * earlier[1] + later[1])


def shards(observations, basis_values, mixing, pattern, decays, loadings):
    owner = lax.axis_index("basis")
    share = mixing.shape[0]
    characteristics = observations.shape[1]
    mixer_rows = block_rows(mixing, pattern, owner)
    rates = decays[0]
    zero_share = jnp.zeros((share, characteristics), jnp.float32)
    identity_pair = (jnp.ones((share,), jnp.float32), zero_share)

    def predict_piece(piece):
        return jnp.dot(basis_values, piece, preferred_element_type=jnp.float32)

    summary = lax.psum_scatter(
        contract_rows(basis_values, observations), "basis", scatter_dimension=0, tiled=True
    )
    mixed_terms = jnp.dot(
        mixer_rows,
        lax.all_gather(summary.astype(jnp.bfloat16), "basis", axis=0, tiled=True),
        preferred_element_type=jnp.float32,
    )
    _, previous = entering((rates, mixed_terms), "region", combine, identity_pair, False)
    states = rates[:, None] * previous + mixed_terms
    loaded_values = (loadings[:, None] * states).astype(jnp.bfloat16)
    fitted = predict_piece(lax.all_gather(loaded_values, "basis", axis=0, tiled=True))
    residual = (fitted - observations.astype(jnp.float32)).astype(jnp.bfloat16)
    pulled = loadings[:, None] * lax.psum_scatter(
        contract_rows(basis_values, residual).astype(jnp.bfloat16),
        "basis",
        scatter_dimension=0,
        tiled=True,
    ).astype(jnp.float32)
    _, carried = entering((rates, rates[:, None] * pulled), "region", combine, identity_pair, True)
    adjoints = pulled + carried
    attenuation_slope = (jnp.sum(adjoints * previous, axis=1) / characteristics)[None, :]
    adjoint_b = adjoints.astype(jnp.bfloat16)
    back_owned = lax.psum_scatter(
        contract_rows(mixer_rows, adjoint_b), "basis", scatter_dimension=0, tiled=True
    ).astype(jnp.bfloat16)
    spread = predict_piece(lax.all_gather(back_owned, "basis", axis=0, tiled=True))
    obs_grad = (spread - residual.astype(jnp.float32)).astype(jnp.bfloat16)
    return (obs_grad, attenuation_slope)


def solution(mesh):
    in_specs = (
        P(("region", "basis"), None),
        P(("region", "basis"), None),
        P("basis", None),
        P(),
        P("region", "basis"),
        P("basis"),
    )
    out_specs = (P(("region", "basis"), None), P("region", "basis"))
    return jax.shard_map(shards, mesh=mesh, in_specs=in_specs, out_specs=out_specs, check_vma=False)
```

profile of v0, /device:TPU:1, one launch (start us, length us, event | category | flops | bytes accessed | tf_op | source)
XLA Modules:
  0.0 245.2 jit_solution(13985293073693226738)
XLA Ops:
  7.2 11.7 %fusion.25 = f32[1024,128]{1,0:T(8,128)} fusion(bf16[8192,1024]{1,0:T(8,128)(2,1)} %param.11, bf16[8192,128]{1,0:T(8,128)(2,1)} %param.10), kind=kOutput, calls=%fused_computation.46 | convolution fusion | flops 2147483648 | bytes 19398656 | tf_op jit(solution)/shard_map/dot_general | solution.py:27
  19.6 23.3 %reduce-scatter.4.cloned.1.call-done = f32[256,128]{1,0:T(8,128)} async-done(((f32[1024,128]{1,0:T(8,128)}), f32[256,128]{1,0:T(8,128)}) %reduce-scatter.4.cloned.1.call-update) | async-done | bytes 131088 | tf_op jit(solution)/shard_map/reduce_scatter | solution.py:61
  43.8 6.3 %all_gather.26 = bf16[1024,128]{1,0:T(8,128)(2,1)S(1)} all-gather(bf16[256,128]{1,0:T(8,128)(2,1)S(1)} %convert_element_type.51), channel_id=1, replica_groups=mesh['region'=8,'basis'=4] {'basis'}, dimensions={0}, use_global_device_ids=true | all-gather | bytes 327680 | tf_op jit(solution)/shard_map/all_gather | solution.py:66
  51.1 2.9 %copy.11 = bf16[8192,128]{0,1:T(8,128)(2,1)} copy(bf16[8192,128]{1,0:T(8,128)(2,1)S(1)} %copy-done.1) | data formatting | bytes 4194304 | tf_op args[0]
  54.0 16.7 %all-gather.2 = f32[8,1,256]{2,1,0:T(1,128)S(1)} all-gather(f32[1,1,256]{2,1,0:T(1,128)S(1)} %bitcast.56), channel_id=1, replica_groups=mesh['region'=8,'basis'=4] {'region'}, dimensions={0}, use_global_device_ids=true | all-gather | bytes 9216 | tf_op jit(solution)/shard_map/all_gather | solution.py:11
  70.7 19.2 %all-gather.6.cloned.1.call-done = f32[2048,128]{1,0:T(8,128)} async-done(((f32[256,128]{1,0:T(8,128)}), f32[2048,128]{1,0:T(8,128)}) %all-gather.6.cloned.1.call-update) | async-done | bytes 1048592 | tf_op jit(solution)/shard_map/all_gather | solution.py:11
  89.9 7.5 %while.28 = (s32[]{:T(128)}, f32[256,128]{1,0:T(8,128)S(1)}, s32[]{:T(128)}, f32[8,256]{1,0:T(8,128)S(1)}, f32[8,256,128]{2,1,0:T(8,128)}, /*index=5*/s32[]{:T(128)}, s32[]{:T(128)}) while((s32[]{:T(128)}, f32[256,128]{1,0:T(8,128)S(1)}, s32[]{:T(128)}, f32[8,256]{1,0:T(8,128)S(1)}, f32[8,256,128]{2,1,0:T(8,128)}, ...), condition=%wide.region_2.3_spmd.clone, body=%wide.region_1.2_spmd.clone.sunk | while | flops 131076 | bytes 396393 | solution.py:23
  91.0 1.0 fusion.40
  92.1 1.0 fusion.40
  93.1 1.0 fusion.40
  94.2 1.0 fusion.40
  97.6 7.5 %all_gather.29 = bf16[1024,128]{1,0:T(8,128)(2,1)S(1)} all-gather(bf16[256,128]{1,0:T(8,128)(2,1)S(1)} %multiply_convert_fusion), channel_id=1, replica_groups=mesh['region'=8,'basis'=4] {'basis'}, dimensions={0}, use_global_device_ids=true | all-gather | bytes 327680 | tf_op jit(solution)/shard_map/all_gather | solution.py:72
  105.0 12.0 %fusion.5 = bf16[8192,128]{0,1:T(8,128)(2,1)S(1)} fusion(bf16[1024,128]{1,0:T(8,128)(2,1)S(1)} %all_gather.29, bf16[8192,1024]{1,0:T(8,128)(2,1)} %param.11, bf16[8192,128]{0,1:T(8,128)(2,1)} %copy.11), kind=kOutput, calls=%fused_computation.11 | convolution fusion | flops 2150629376 | bytes 21233664 | tf_op jit(solution)/shard_map/dot_general | solution.py:59
  117.1 10.8 %fusion.8 = bf16[1024,128]{1,0:T(8,128)(2,1)} fusion(bf16[8192,128]{0,1:T(8,128)(2,1)S(1)} %fusion.5, bf16[8192,1024]{1,0:T(8,128)(2,1)} %param.11), kind=kOutput, calls=%fused_computation.16 | convolution fusion | flops 2147614720 | bytes 19136512 | tf_op jit(solution)/shard_map/dot_general | solution.py:27
  128.0 18.4 %reduce-scatter.6.cloned.1.call-done = bf16[256,128]{1,0:T(8,128)(2,1)} async-done(((bf16[1024,128]{1,0:T(8,128)(2,1)}), bf16[256,128]{1,0:T(8,128)(2,1)}) %reduce-scatter.6.cloned.1.call-update) | async-done | bytes 65552 | tf_op jit(solution)/shard_map/reduce_scatter | solution.py:74
  146.3 1.7 fusion.13
  148.2 39.9 %all-gather.8.cloned.1.call-done = f32[2048,128]{1,0:T(8,128)} async-done(((f32[256,128]{1,0:T(8,128)}), f32[2048,128]{1,0:T(8,128)}) %all-gather.8.cloned.1.call-update) | async-done | bytes 1048592 | tf_op jit(solution)/shard_map/all_gather | solution.py:11
  188.1 1.3 rev.7
  189.4 1.1 while.29
  190.6 2.2 fusion.15
  193.6 20.8 %reduce-scatter.8.cloned.1.call-done = f32[256,128]{1,0:T(8,128)} async-done(((f32[1024,128]{1,0:T(8,128)}), f32[256,128]{1,0:T(8,128)}) %reduce-scatter.8.cloned.1.call-update) | async-done | bytes 131088 | tf_op jit(solution)/shard_map/reduce_scatter | solution.py:84
  215.3 6.5 %all_gather.32 = bf16[1024,128]{1,0:T(8,128)(2,1)S(1)} all-gather(bf16[256,128]{1,0:T(8,128)(2,1)S(1)} %convert_element_type.59), channel_id=1, replica_groups=mesh['region'=8,'basis'=4] {'basis'}, dimensions={0}, use_global_device_ids=true | all-gather | bytes 327680 | tf_op jit(solution)/shard_map/all_gather | solution.py:87
  221.9 12.8 %fusion.4 = bf16[8192,128]{0,1:T(8,128)(2,1)} fusion(bf16[1024,128]{1,0:T(8,128)(2,1)S(1)} %all_gather.32, bf16[8192,1024]{1,0:T(8,128)(2,1)} %param.11, bf16[8192,128]{0,1:T(8,128)(2,1)S(1)} %fusion.5), kind=kOutput, calls=%fused_computation.10 | convolution fusion | flops 2150629376 | bytes 21233664 | tf_op jit(solution)/shard_map/dot_general | solution.py:59
  234.6 4.1 %copy.13 = bf16[8192,128]{1,0:T(8,128)(2,1)} copy(bf16[8192,128]{0,1:T(8,128)(2,1)} %fusion.4) | data formatting | bytes 4194304
  (63 shorter events, 8.6 us)
Async XLA Ops:
  7.2 11.9 %copy-start.6 = (bf16[256,1024]{1,0:T(8,128)(2,1)S(1)}, bf16[256,1024]{1,0:T(8,128)(2,1)}, u32[]{:S(2)}) copy-start(bf16[256,1024]{1,0:T(8,128)(2,1)} %param.12) | copy-start | bytes 1572868
  7.2 11.9 %copy-start.7 = (s32[8,8]{1,0:T(8,128)S(1)}, s32[8,8]{1,0:T(8,128)}, u32[]{:S(2)}) copy-start(s32[8,8]{1,0:T(8,128)} %param.13) | copy-start | bytes 772
  7.2 35.7 %reduce-scatter.4.cloned.1.call-start = ((), (), s32[]{:S(2)}) async-start(), calls=%async_computation.3 | async-start | bytes 655360 | tf_op jit(solution)/shard_map/reduce_scatter | solution.py:61
  18.9 32.2 %copy-start.1 = (bf16[8192,128]{1,0:T(8,128)(2,1)S(1)}, bf16[8192,128]{1,0:T(8,128)(2,1)}, u32[]{:S(2)}) copy-start(bf16[8192,128]{1,0:T(8,128)(2,1)} %param.10) | copy-start | bytes 6291460
  18.9 35.1 %copy-start.5 = (f32[1,256]{1,0:T(1,128)S(1)}, f32[1,256]{1,0:T(1,128)}, u32[]{:S(2)}) copy-start(f32[1,256]{1,0:T(1,128)} %param.14) | copy-start | bytes 3076
  19.0 71.0 %all-gather.6.cloned.1.call-start = ((), (), s32[]{:S(2)}) async-start(), calls=%async_computation.6 | async-start | bytes 1179648 | tf_op jit(solution)/shard_map/all_gather | solution.py:11
  19.6 31.4 %copy-start = (bf16[256,1024]{1,0:T(8,128)(2,1)}, bf16[256,1024]{1,0:T(8,128)(2,1)S(1)}, u32[]{:S(2)}) copy-start(bf16[256,1024]{1,0:T(8,128)(2,1)S(1)} %fusion.7) | copy-start | bytes 1572868
  19.6 77.8 %copy-start.4 = (f32[256]{0:T(256)S(1)}, f32[256]{0:T(256)}, u32[]{:S(2)}) copy-start(f32[256]{0:T(256)} %param.15) | copy-start | bytes 3076
  51.0 46.4 %copy-start.2 = (f32[256,128]{1,0:T(8,128)S(1)}, f32[256,128]{1,0:T(8,128)}, u32[]{:S(2)}) copy-start(f32[256,128]{1,0:T(8,128)} %fusion.26) | copy-start | bytes 393220
  51.0 95.3 %reduce-scatter.6.cloned.1.call-start = ((), (), s32[]{:S(2)}) async-start(), calls=%async_computation.4 | async-start | bytes 327680 | tf_op jit(solution)/shard_map/reduce_scatter | solution.py:74
  127.9 60.2 %all-gather.8.cloned.1.call-start = ((), (), s32[]{:S(2)}) async-start(), calls=%async_computation.7 | async-start | bytes 1179648 | tf_op jit(solution)/shard_map/all_gather | solution.py:11
  146.3 44.2 %copy-start.3 = (bf16[256,128]{1,0:T(8,128)(2,1)S(1)}, bf16[256,128]{1,0:T(8,128)(2,1)}, u32[]{:S(2)}) copy-start(bf16[256,128]{1,0:T(8,128)(2,1)} %reduce-scatter.6.cloned.1.call-done) | copy-start | bytes 196612
  148.1 66.4 %reduce-scatter.8.cloned.1.call-start = ((), (), s32[]{:S(2)}) async-start(), calls=%async_computation.5 | async-start | bytes 655360 | tf_op jit(solution)/shard_map/reduce_scatter | solution.py:84
Sparse Core Ops, SparseCore 0:
  19.1 23.7 reduce-scatter.3
  51.1 38.7 all-gather.5
  128.0 18.2 reduce-scatter.5
  148.9 39.1 all-gather.7
  193.0 21.4 reduce-scatter.7
where the time goes:
time: 246 us; the launch traced here: 245 us
  waiting for transfers between devices  122 us (50%)
  matrix products  51 us (21%)
  blocking collectives  37 us (15%)
  between operations  14 us (6%)
  other arithmetic  12.5 us (5%)
  local copies, waits for them, and re-layouts  8.45 us (3%)
    all_gather x2, waiting for transfers between devices, entering(): pieces = jax.tree.map(lambda part: lax.all_gather(part, axis), value)  59.1 us
    dot_general x2, matrix products, predict_piece(): return jnp.dot(basis_values, piece, preferred_element_type=jnp.float32)  24.8 us
    dot_general x3, matrix products, contract_rows(): lax.dot_general(first_operand, second_operand, (((0,), (0,)), ((), ())),...  24.8 us
    reduce_scatter x1, waiting for transfers between devices, shards(): lax.psum_scatter(contract_rows(basis_values, observations), 'basis', scat...  23.3 us
    reduce_scatter x1, waiting for transfers between devices, shards(): lax.psum_scatter(contract_rows(mixer_rows, adjoint_b), 'basis', scatter_d...  20.8 us
    reduce_scatter x1, waiting for transfers between devices, shards(): lax.psum_scatter(contract_rows(basis_values, residual).astype(jnp.bfloat1...  18.4 us
    all_gather x1, blocking collectives, entering(): pieces = jax.tree.map(lambda part: lax.all_gather(part, axis), value)  16.7 us
    select_n x14, other arithmetic, turn(): jnp.where(position < mine, new, old)  8.05 us
  transfers between devices with their start and end apart: 5, of which 5 were waited for; matrix products, arithmetic and copies ran while one was open for 2% of the time, Pallas kernels for 0%

commit v1 on v0

v1 whole, which is shorter than its diff:
```python
import functools
import math
import jax
import jax.numpy as jnp
from jax import lax
from jax.experimental import pallas as pl
from jax.experimental.pallas import tpu as pltpu
from jax.sharding import PartitionSpec as P

BLOCK = 128
CHUNKS = 8
MESH = pl.DeviceIdType.MESH


def flip(index, mask, count):
    total = 0
    for k in range(count.bit_length() - 1):
        bit = lax.rem(lax.div(index, 1 << k), 2)
        total = total + (bit if not (mask >> k) & 1 else 1 - bit) * (1 << k)
    return total


def fan_order(count):
    return sorted(range(1, count), key=lambda m: (bin(m).count("1"), -m))


def kernel(n, nr, y_hbm, phi_hbm, mix_hbm, pattern, decays, loadings, out_hbm, slope,
           phi, y, yt, mixraw, mixer, wide, rs_src, rs_dst, gathered, a_src, a_dst, s_src, s_dst,
           phi_sem, y_sem, mix_sem, out_sem, rs_send, rs_recv, ag_send, ag_recv,
           mx_send, mx_recv, a_send, a_recv, s_send, s_recv):
    b, r = lax.axis_index("basis"), lax.axis_index("region")
    steps = nr.bit_length() - 1
    _, chunks, tall, width = phi.shape
    traits = y.shape[2]
    per = width // BLOCK
    f32, bf16 = jnp.float32, jnp.bfloat16
    mate = [flip(b, m, n) for m in range(n)]
    across = [flip(r, 1 << k, nr) for k in range(steps)]
    order = list(range(n - 1, -1, -1))

    def phi_copy(m, c):
        return pltpu.make_async_copy(
            phi_hbm.at[pl.ds(pl.multiple_of(c * tall, tall), tall),
                       pl.ds(pl.multiple_of(mate[m] * width, width), width)],
            phi.at[m, c], phi_sem.at[m, c])

    def y_copy(c):
        return pltpu.make_async_copy(
            y_hbm.at[pl.ds(pl.multiple_of(c * tall, tall), tall), :], y.at[c], y_sem.at[c])

    def mix_copy(m):
        return pltpu.make_async_copy(
            mix_hbm.at[:, pl.ds(pl.multiple_of(mate[m] * width, width), width)],
            mixraw.at[m], mix_sem.at[m])

    def out_copy(c):
        return pltpu.make_async_copy(
            y.at[c], out_hbm.at[pl.ds(pl.multiple_of(c * tall, tall), tall), :], out_sem.at[c])

    for position, m in enumerate(order):
        @pl.loop(0, chunks)
        def _(c):
            if position == 0:
                y_copy(c).start()
            phi_copy(m, c).start()
        if position == 0:
            for other in range(n):
                mix_copy(other).start()

    barrier = pltpu.get_barrier_semaphore()
    for m in range(1, n):
        pl.semaphore_signal(barrier, inc=1, device_id={"basis": mate[m]}, device_id_type=MESH)
    for k in range(steps):
        pl.semaphore_signal(barrier, inc=1, device_id={"region": across[k]}, device_id_type=MESH)
    pl.semaphore_wait(barrier, n - 1 + steps)

    started = []

    def send(copy):
        copy.start()
        started.append(copy)

    def to_mate(src, dst, send_sem, recv_sem, m):
        return pltpu.make_async_remote_copy(
            src_ref=src, dst_ref=dst, send_sem=send_sem, recv_sem=recv_sem,
            device_id={"basis": mate[m]}, device_id_type=MESH)

    def to_across(src, dst, send_sem, recv_sem, k):
        return pltpu.make_async_remote_copy(
            src_ref=src, dst_ref=dst, send_sem=send_sem, recv_sem=recv_sem,
            device_id={"region": across[k]}, device_id_type=MESH)

    def gather_copy(use, m):
        low = m & -m
        return to_mate(gathered.at[use, m ^ low], gathered.at[use, m],
                       ag_send.at[use, m], ag_recv.at[use, m], low)

    def gather(use, consume):
        ready = {0}
        plan = fan_order(n)
        for m in plan:
            if bin(m).count("1") == 1:
                send(gather_copy(use, m))
        consume(0)
        for m in plan:
            source = m ^ (m & -m)
            if bin(m).count("1") > 1:
                if source not in ready:
                    gather_copy(use, source).wait_recv()
                    ready.add(source)
                send(gather_copy(use, m))
        for m in range(1, n):
            if m not in ready:
                gather_copy(use, m).wait_recv()
                ready.add(m)
            consume(m)

    def mixer_copy(m, j):
        low = m & -m
        return to_mate(mixer.at[m ^ low, j ^ low], mixer.at[m, j],
                       mx_send.at[m, j], mx_recv.at[m, j], low)

    def part_copy(use, m):
        return to_mate(rs_src.at[use, m], rs_dst.at[use, m],
                       rs_send.at[use, m], rs_recv.at[use, m], m)

    def rate_copy(k):
        return to_across(a_src.at[k], a_dst.at[k], a_send.at[k], a_recv.at[k], k)

    def scan_copy(use, k):
        return to_across(s_src.at[use, k], s_dst.at[use, k],
                         s_send.at[use, k], s_recv.at[use, k], k)

    rate = decays[...]
    load = loadings[...]
    ones = jnp.ones_like(rate)
    rates = {"own": rate, "before": ones, "after": ones}
    factors = []

    def rate_start(k):
        a_src[k] = jnp.broadcast_to(rates["own"], a_src.shape[1:])
        send(rate_copy(k))

    def rate_end(k):
        rate_copy(k).wait_recv()
        own, theirs = rates["own"], a_dst[k][0:1, :]
        before, after = rates["before"], rates["after"]
        up = jnp.full(rate.shape, lax.rem(lax.div(r, 1 << k), 2)) == 1
        factors.append((
            (jnp.where(up, 1.0, theirs), jnp.where(up, own, 1.0), jnp.where(up, before, 0.0)),
            (jnp.where(up, theirs, 1.0), jnp.where(up, 1.0, own), jnp.where(up, 0.0, after)),
        ))
        rates["before"] = jnp.where(up, theirs * before, before)
        rates["after"] = jnp.where(up, after, theirs * after)
        rates["own"] = own * theirs

    def scan(use, total):
        carried = jnp.zeros_like(total)
        for k in range(steps):
            s_src[use, k] = total.astype(bf16)
            send(scan_copy(use, k))
            keep, take, enter = factors[k][use]
            scan_copy(use, k).wait_recv()
            other = s_dst[use, k].astype(f32)
            carried = carried + enter * other
            total = keep * total + take * other
        return carried

    def build_mixer():
        rows = lax.broadcasted_iota(jnp.int32, (BLOCK, BLOCK), 0)
        columns = lax.broadcasted_iota(jnp.int32, (BLOCK, BLOCK), 1)
        eye = jnp.where(rows == columns, 1.0, 0.0).astype(f32)
        for m in range(n):
            mix_copy(m).wait()
            for i in range(per):
                for j in range(per):
                    at = (m, pl.ds(i * BLOCK, BLOCK), pl.ds(j * BLOCK, BLOCK))
                    present = pattern[b * per + i, mate[m] * per + j].astype(f32)
                    entry = mixraw[at].astype(f32) * present
                    if m == 0 and i == j:
                        entry = entry + eye
                    mixer[(0,) + at] = entry.astype(bf16)

    def turned(block):
        return block.astype(f32).T.astype(bf16)

    def project(use):
        for position, m in enumerate(order):
            def body(c, total):
                if use == 0:
                    if position == 0:
                        y_copy(c).wait()
                        yt[c] = turned(y[c])
                    phi_copy(m, c).wait()
                return total + jnp.dot(yt[c], phi[m, c], preferred_element_type=f32)

            total = lax.fori_loop(0, chunks, body, jnp.zeros((traits, width), f32))
            if m:
                rs_src[use, m] = total.astype(bf16)
                send(part_copy(use, m))
            if use == 0:
                if position == 0:
                    build_mixer()
                if position < steps:
                    rate_end(position)
                    if position + 1 < steps:
                        rate_start(position + 1)
        for m in order[:-1]:
            part_copy(use, m).wait_recv()
            total = total + rs_dst[use, m].astype(f32)
        return total

    rate_start(0)
    summary = project(0)
    for k in range(n, steps):
        rate_end(k)
        if k + 1 < steps:
            rate_start(k + 1)

    gathered[0, 0] = summary.astype(bf16)
    sums = []

    def mix_in(m):
        sums.append(lax.dot_general(gathered[0, m], mixer[0, m], (((1,), (1,)), ((), ())),
                                    preferred_element_type=f32))

    gather(0, mix_in)
    mixed = functools.reduce(jnp.add, sums)

    plan = fan_order(n)
    direct = [m for m in plan if bin(m).count("1") == 1]
    half = n // 2
    for m in direct:
        for j in range(half):
            send(mixer_copy(m, j))

    previous = scan(0, mixed)
    state = rate * previous + mixed
    gathered[1, 0] = (load * state).astype(bf16)

    def widen(m):
        wide[m] = turned(gathered[1, m])

    gather(1, widen)
    for m in direct:
        for j in range(half, n):
            send(mixer_copy(m, j))

    def predict(c):
        total = jnp.dot(phi[0, c], wide[0], preferred_element_type=f32)
        for m in range(1, n):
            total = total + jnp.dot(phi[m, c], wide[m], preferred_element_type=f32)
        return total

    @pl.loop(0, chunks)
    def _(c):
        residual = predict(c) - y[c].astype(f32)
        y[c] = residual.astype(bf16)
        yt[c] = residual.T.astype(bf16)

    seen = set()

    def mixer_there(m):
        if m and m not in seen:
            for j in range(n):
                mixer_copy(m, j).wait_recv()
            seen.add(m)

    for m in plan:
        if m not in direct:
            mixer_there(m ^ (m & -m))
            for j in range(n):
                send(mixer_copy(m, j))

    pulled = load * project(1)
    adjoint = pulled + scan(1, rate * pulled)
    gathered[2, 0] = adjoint.astype(bf16)
    slope[...] = jnp.sum(adjoint * previous, axis=0, keepdims=True) / traits
    backs = [jnp.zeros((traits, width), f32) for _ in range(n)]

    def mix_back(m):
        mixer_there(m)
        for j in range(n):
            backs[j] = backs[j] + jnp.dot(gathered[2, m], mixer[m, j], preferred_element_type=f32)

    gather(2, mix_back)
    for j in range(n):
        wide[j] = backs[j].T.astype(bf16)

    @pl.loop(0, chunks)
    def _(c):
        y[c] = (predict(c) - y[c].astype(f32)).astype(bf16)
        out_copy(c).start()

    for copy in started:
        copy.wait_send()

    @pl.loop(0, chunks)
    def _(c):
        out_copy(c).wait()


def shards(n, nr, observations, basis_values, mixing, pattern, decays, loadings):
    rows, traits = observations.shape
    width = mixing.shape[0]
    steps = nr.bit_length() - 1
    chunks, tall = CHUNKS, rows // CHUNKS
    f32, bf16 = jnp.float32, jnp.bfloat16
    dma = pltpu.SemaphoreType.DMA
    hbm = pl.BlockSpec(memory_space=pl.ANY)
    vmem = pl.BlockSpec(memory_space=pltpu.VMEM)
    return pl.pallas_call(
        functools.partial(kernel, n, nr),
        out_shape=(jax.ShapeDtypeStruct((rows, traits), bf16),
                   jax.ShapeDtypeStruct((1, width), f32)),
        in_specs=[hbm, hbm, hbm, pl.BlockSpec(memory_space=pltpu.SMEM), vmem, vmem],
        out_specs=(hbm, vmem),
        scratch_shapes=[
            pltpu.VMEM((n, chunks, tall, width), bf16),
            pltpu.VMEM((chunks, tall, traits), bf16),
            pltpu.VMEM((chunks, traits, tall), bf16),
            pltpu.VMEM((n, width, width), bf16),
            pltpu.VMEM((n, n, width, width), bf16),
            pltpu.VMEM((n, width, traits), bf16),
            pltpu.VMEM((2, n, traits, width), bf16),
            pltpu.VMEM((2, n, traits, width), bf16),
            pltpu.VMEM((3, n, traits, width), bf16),
            pltpu.VMEM((steps, 8, width), f32),
            pltpu.VMEM((steps, 8, width), f32),
            pltpu.VMEM((2, steps, traits, width), bf16),
            pltpu.VMEM((2, steps, traits, width), bf16),
            dma((n, chunks)), dma((chunks,)), dma((n,)), dma((chunks,)),
            dma((2, n)), dma((2, n)), dma((3, n)), dma((3, n)),
            dma((n, n)), dma((n, n)), dma((steps,)), dma((steps,)),
            dma((2, steps)), dma((2, steps)),
        ],
        compiler_params=pltpu.CompilerParams(
            collective_id=0, has_side_effects=True, vmem_limit_bytes=48 * 2**20),
        cost_estimate=pl.CostEstimate(
            flops=8 * rows * n * width * traits, transcendentals=0,
            bytes_accessed=2 * rows * (n * width + 2 * traits)),
    )(observations, basis_values, mixing, pattern, decays, loadings.reshape(1, width))


def solution(mesh):
    in_specs = (
        P(("region", "basis"), None),
        P(("region", "basis"), None),
        P("basis", None),
        P(),
        P("region", "basis"),
        P("basis"),
    )
    out_specs = (P(("region", "basis"), None), P("region", "basis"))
    body = functools.partial(shards, mesh.shape["basis"], mesh.shape["region"])
    return jax.shard_map(body, mesh=mesh, in_specs=in_specs, out_specs=out_specs, check_vma=False)
```

time: 246 us -> 81.6 us (0.33)
  waiting for transfers between devices: 122 us -> 0 us
  Pallas kernels: 0 us -> 74.1 us
  matrix products: 51 us -> 0 us
  blocking collectives: 37 us -> 0 us
  between operations: 14 us -> 0.65 us
  other arithmetic: 12.5 us -> 0 us
    pallas_call x0 -> x1, Pallas kernels: none -> 74.1 us  [shards(): pl.pallas_call(functools.partial(kernel, n, nr), out_shape=(jax.ShapeDtyp...]
    reduce_scatter x3 -> x0, waiting for transfers between devices: 62.4 us -> none  [the longest x1 23.3 us: shards(): lax.psum_scatter(contract_rows(basis_values, observations), 'basis', scat...]
    all_gather x2 -> x0, waiting for transfers between devices: 59.1 us -> none  [entering(): pieces = jax.tree.map(lambda part: lax.all_gather(part, axis), value)]
    dot_general x7 -> x0, matrix products: 51 us -> none  [the longest x2 24.8 us: predict_piece(): return jnp.dot(basis_values, piece, preferred_element_type=jnp.float32)]
    all_gather x4 -> x0, blocking collectives: 37 us -> none  [the longest x1 16.7 us: entering(): pieces = jax.tree.map(lambda part: lax.all_gather(part, axis), value)]
    select_n x16 -> x0, other arithmetic: 8.06 us -> none  [the longest x14 8.05 us: turn(): jnp.where(position < mine, new, old)]
    unnamed x19 -> x12, local copies, waits for them, and re-layouts: 6.99 us -> 6.55 us
  transfers between devices with their start and end apart: 5 -> 0, of which waited for: 5 -> 0; matrix products, arithmetic and copies ran while one was open for 2% -> 0% of each run, Pallas kernels for 0% -> 0%
where the time goes in v1:
time: 81.6 us; the launch traced here: 81.3 us
  Pallas kernels  74.1 us (91%)
  local copies, waits for them, and re-layouts  6.55 us (8%)
    pallas_call x1, Pallas kernels, shards(): pl.pallas_call(functools.partial(kernel, n, nr), out_shape=(jax.ShapeDtyp...  74.1 us
    unnamed x12, local copies, waits for them, and re-layouts  6.55 us

profile of v1, /device:TPU:1, one launch (start us, length us, event | category | flops | bytes accessed | tf_op | source)
XLA Modules:
  0.0 81.3 jit_solution(2227252548500863430)
XLA Ops:
  0.6 0.0 copy-start
  0.6 1.6 %copy-done = bf16[8192,128]{1,0:T(8,128)(2,1)S(1)} copy-done((bf16[8192,128]{1,0:T(8,128)(2,1)S(1)}, bf16[8192,128]{1,0:T(8,128)(2,1)}, u32[]{:S(2)}) %copy-start) | copy-done | bytes 2097176
  2.2 0.0 copy-start.1
  2.2 1.0 %copy-done.1 = bf16[256,1024]{1,0:T(8,128)(2,1)S(1)} copy-done((bf16[256,1024]{1,0:T(8,128)(2,1)S(1)}, bf16[256,1024]{1,0:T(8,128)(2,1)}, u32[]{:S(2)}) %copy-start.1) | copy-done | bytes 524312
  3.3 0.0 copy-start.2
  3.3 0.7 copy-done.2
  4.0 0.0 copy-start.3
  4.0 0.7 copy-done.3
  4.6 0.0 copy-start.4
  4.6 0.7 copy-done.4
  5.3 74.1 %shard_map.77 = (bf16[8192,128]{1,0:T(8,128)(2,1)S(1)}, f32[1,256]{1,0:T(1,128)S(1)}) custom-call(bf16[8192,128]{1,0:T(8,128)(2,1)S(1)} %copy-done, bf16[8192,1024]{1,0:T(8,128)(2,1)} %phi_hbm.1, bf16[256,1024]{1,0:T(8,128)(2,1)S(1)} %copy-done.1, s32[8,8]{1,0:T(8,128)S(1)} %copy-done.2, f32[1,256]{1,0:T(1,128)S(1)} %copy-done.3, f32[1,256]{1,0:T(1,128)S(1)} %bitcast.1), custom_call_target="tpu_custom_call" | custom-call | flops 8589934592 | bytes 20971520 | tf_op jit(solution)/shard_map/pallas_call | solution.py:312
  79.4 1.3 %copy.10 = bf16[8192,128]{1,0:T(8,128)(2,1)} copy(bf16[8192,128]{1,0:T(8,128)(2,1)S(1)} %get-tuple-element.4) | data formatting | bytes 4194304
  80.8 0.6 copy.11
Async XLA Ops:
  0.6 1.6 %copy-start = (bf16[8192,128]{1,0:T(8,128)(2,1)S(1)}, bf16[8192,128]{1,0:T(8,128)(2,1)}, u32[]{:S(2)}) copy-start(bf16[8192,128]{1,0:T(8,128)(2,1)} %y_hbm.1) | copy-start | bytes 6291460
  2.2 1.0 %copy-start.1 = (bf16[256,1024]{1,0:T(8,128)(2,1)S(1)}, bf16[256,1024]{1,0:T(8,128)(2,1)}, u32[]{:S(2)}) copy-start(bf16[256,1024]{1,0:T(8,128)(2,1)} %mix_hbm.1) | copy-start | bytes 1572868
  3.3 0.7 copy-start.2
  4.0 0.7 copy-start.3
  4.6 0.7 copy-start.4

commit v2 on v1

--- a/solution.py
+++ b/solution.py
@@ -24,25 +24,32 @@
     return sorted(range(1, count), key=lambda m: (bin(m).count("1"), -m))
 
 
-def kernel(n, nr, y_hbm, phi_hbm, mix_hbm, pattern, decays, loadings, out_hbm, slope,
+def kernel(n, nr, y_hbm, phi_hbm, mix_hbm, pattern_hbm, decays_hbm, loadings_hbm, out_hbm, slope,
            phi, y, yt, mixraw, mixer, wide, rs_src, rs_dst, gathered, a_src, a_dst, s_src, s_dst,
+           pattern, decays, loadings, parts, gram_row, gram,
            phi_sem, y_sem, mix_sem, out_sem, rs_send, rs_recv, ag_send, ag_recv,
-           mx_send, mx_recv, a_send, a_recv, s_send, s_recv):
+           mx_send, mx_recv, a_send, a_recv, s_send, s_recv, small_sem):
     b, r = lax.axis_index("basis"), lax.axis_index("region")
     steps = nr.bit_length() - 1
-    _, chunks, tall, width = phi.shape
+    chunks, tall, _ = phi.shape
+    width = mixraw.shape[1]
     traits = y.shape[2]
     per = width // BLOCK
     f32, bf16 = jnp.float32, jnp.bfloat16
     mate = [flip(b, m, n) for m in range(n)]
     across = [flip(r, 1 << k, nr) for k in range(steps)]
     order = list(range(n - 1, -1, -1))
+    half = n // 2
+
+    def block(m, count=1):
+        return pl.ds(m * width, count * width)
+
 
     def phi_copy(m, c):
         return pltpu.make_async_copy(
             phi_hbm.at[pl.ds(pl.multiple_of(c * tall, tall), tall),
                        pl.ds(pl.multiple_of(mate[m] * width, width), width)],
-            phi.at[m, c], phi_sem.at[m, c])
+            phi.at[c, :, block(m)], phi_sem.at[m, c])
 
     def y_copy(c):
         return pltpu.make_async_copy(
@@ -57,13 +64,18 @@
         return pltpu.make_async_copy(
             y.at[c], out_hbm.at[pl.ds(pl.multiple_of(c * tall, tall), tall), :], out_sem.at[c])
 
-    for position, m in enumerate(order):
+    small = [pltpu.make_async_copy(src, dst, small_sem.at[at]) for at, (src, dst) in enumerate(
+        ((decays_hbm, decays), (loadings_hbm, loadings), (pattern_hbm, pattern)))]
+    for copy in small:
+        copy.start()
+    for first in (half, 0):
         @pl.loop(0, chunks)
         def _(c):
-            if position == 0:
+            if first:
                 y_copy(c).start()
-            phi_copy(m, c).start()
-        if position == 0:
+            for m in range(first, first + half):
+                phi_copy(m, c).start()
+        if first:
             for other in range(n):
                 mix_copy(other).start()
 
@@ -95,7 +107,7 @@
         return to_mate(gathered.at[use, m ^ low], gathered.at[use, m],
                        ag_send.at[use, m], ag_recv.at[use, m], low)
 
-    def gather(use, consume):
+    def gather(use, consume, work=lambda: None):
         ready = {0}
         plan = fan_order(n)
         for m in plan:
@@ -106,11 +118,14 @@
             source = m ^ (m & -m)
             if bin(m).count("1") > 1:
                 if source not in ready:
+                    work()
                     gather_copy(use, source).wait_recv()
                     ready.add(source)
                 send(gather_copy(use, m))
         for m in range(1, n):
             if m not in ready:
+                if m == n - 1:
+                    work()
                 gather_copy(use, m).wait_recv()
                 ready.add(m)
             consume(m)
@@ -131,6 +146,8 @@
         return to_across(s_src.at[use, k], s_dst.at[use, k],
                          s_send.at[use, k], s_recv.at[use, k], k)
 
+    for copy in small:
+        copy.wait()
     rate = decays[...]
     load = loadings[...]
     ones = jnp.ones_like(rate)
@@ -154,12 +171,13 @@
         rates["after"] = jnp.where(up, after, theirs * after)
         rates["own"] = own * theirs
 
-    def scan(use, total):
+    def scan(use, total, work=lambda: None):
         carried = jnp.zeros_like(total)
         for k in range(steps):
             s_src[use, k] = total.astype(bf16)
             send(scan_copy(use, k))
             keep, take, enter = factors[k][use]
+            work()
             scan_copy(use, k).wait_recv()
             other = s_dst[use, k].astype(f32)
             carried = carried + enter * other
@@ -184,80 +202,111 @@
     def turned(block):
         return block.astype(f32).T.astype(bf16)
 
-    def project(use):
-        for position, m in enumerate(order):
-            def body(c, total):
-                if use == 0:
-                    if position == 0:
-                        y_copy(c).wait()
-                        yt[c] = turned(y[c])
-                    phi_copy(m, c).wait()
-                return total + jnp.dot(yt[c], phi[m, c], preferred_element_type=f32)
-
-            total = lax.fori_loop(0, chunks, body, jnp.zeros((traits, width), f32))
-            if m:
-                rs_src[use, m] = total.astype(bf16)
-                send(part_copy(use, m))
-            if use == 0:
-                if position == 0:
-                    build_mixer()
-                if position < steps:
-                    rate_end(position)
-                    if position + 1 < steps:
-                        rate_start(position + 1)
+    def send_part(use, m, value):
+        rs_src[use, m] = value.astype(bf16)
+        send(part_copy(use, m))
+
+    def owned(use, total):
         for m in order[:-1]:
             part_copy(use, m).wait_recv()
             total = total + rs_dst[use, m].astype(f32)
         return total
 
+    def project():
+        for first in (half, 0):
+            def body(c, total):
+                if first:
+                    y_copy(c).wait()
+                    yt[c] = turned(y[c])
+                for m in range(first, first + half):
+                    phi_copy(m, c).wait()
+                return total + jnp.dot(yt[c], phi[c, :, block(first, half)],
+                                       preferred_element_type=f32)
+
+            total = lax.fori_loop(0, chunks, body, jnp.zeros((traits, half * width), f32))
+            for m in reversed(range(first, first + half)):
+                parts[m] = total[:, (m - first) * width:(m - first + 1) * width]
+                if m:
+                    send_part(0, m, parts[m])
+            if first:
+                build_mixer()
+            for k in range(0 if first else 1, 1 if first else steps):
+                rate_end(k)
+                if k + 1 < steps:
+                    rate_start(k + 1)
+
+    def gram_piece(m, start, stop):
+        span = block(m, n - m)
+
+        def piece():
+            if start == 0:
+                gram_row[:, span] = jnp.zeros((width, (n - m) * width), f32)
+
+            @pl.loop(start, stop)
+            def _(c):
+                gram_row[:, span] += lax.dot_general(
+                    phi[c, :, block(m)], phi[c, :, span], (((0,), (0,)), ((), ())),
+                    preferred_element_type=f32)
+
+            if stop == chunks:
+                for other in range(m, n):
+                    found = gram_row[:, block(other)]
+                    gram[m, other] = found.astype(bf16)
+                    if other != m:
+                        gram[other, m] = found.T.astype(bf16)
+        return piece
+
+    cuts = {0: (0, 3, 6, chunks), 1: (0, 4, chunks)}
+    pieces = []
+    for m in range(n):
+        cut = cuts.get(m, (0, chunks))
+        pieces += [gram_piece(m, *ends) for ends in zip(cut[:-1], cut[1:])]
+
+    def work():
+        if pieces:
+            pieces.pop(0)()
+
     rate_start(0)
-    summary = project(0)
-    for k in range(n, steps):
-        rate_end(k)
-        if k + 1 < steps:
-            rate_start(k + 1)
-
-    gathered[0, 0] = summary.astype(bf16)
+    project()
+    work()
+    gathered[0, 0] = owned(0, parts[0]).astype(bf16)
     sums = []
 
     def mix_in(m):
         sums.append(lax.dot_general(gathered[0, m], mixer[0, m], (((1,), (1,)), ((), ())),
                                     preferred_element_type=f32))
 
-    gather(0, mix_in)
+    gather(0, mix_in, work)
     mixed = functools.reduce(jnp.add, sums)
 
     plan = fan_order(n)
     direct = [m for m in plan if bin(m).count("1") == 1]
-    half = n // 2
     for m in direct:
         for j in range(half):
             send(mixer_copy(m, j))
 
-    previous = scan(0, mixed)
+    previous = scan(0, mixed, work)
     state = rate * previous + mixed
     gathered[1, 0] = (load * state).astype(bf16)
-
-    def widen(m):
-        wide[m] = turned(gathered[1, m])
-
-    gather(1, widen)
+    gather(1, lambda m: None, work)
+    while pieces:
+        work()
+
+    for m in order:
+        pull = -parts[m]
+        for other in range(n):
+            pull = pull + jnp.dot(gathered[1, other], gram[other, m], preferred_element_type=f32)
+        if m:
+            send_part(1, m, pull)
+    pulled = load * owned(1, pull)
+
     for m in direct:
         for j in range(half, n):
             send(mixer_copy(m, j))
-
-    def predict(c):
-        total = jnp.dot(phi[0, c], wide[0], preferred_element_type=f32)
-        for m in range(1, n):
-            total = total + jnp.dot(phi[m, c], wide[m], preferred_element_type=f32)
-        return total
-
-    @pl.loop(0, chunks)
-    def _(c):
-        residual = predict(c) - y[c].astype(f32)
-        y[c] = residual.astype(bf16)
-        yt[c] = residual.T.astype(bf16)
-
+    adjoint = pulled + scan(1, rate * pulled)
+    gathered[2, 0] = adjoint.astype(bf16)
+    slope[...] = jnp.sum(adjoint * previous, axis=0, keepdims=True) / traits
+    backs = [-gathered[1, j].astype(f32) for j in range(n)]
     seen = set()
 
     def mixer_there(m):
@@ -266,30 +315,25 @@
                 mixer_copy(m, j).wait_recv()
             seen.add(m)
 
-    for m in plan:
-        if m not in direct:
-            mixer_there(m ^ (m & -m))
-            for j in range(n):
-                send(mixer_copy(m, j))
-
-    pulled = load * project(1)
-    adjoint = pulled + scan(1, rate * pulled)
-    gathered[2, 0] = adjoint.astype(bf16)
-    slope[...] = jnp.sum(adjoint * previous, axis=0, keepdims=True) / traits
-    backs = [jnp.zeros((traits, width), f32) for _ in range(n)]
-
     def mix_back(m):
+        if m == 0:
+            for other in plan:
+                if other not in direct:
+                    mixer_there(other ^ (other & -other))
+                    for j in range(n):
+                        send(mixer_copy(other, j))
         mixer_there(m)
         for j in range(n):
             backs[j] = backs[j] + jnp.dot(gathered[2, m], mixer[m, j], preferred_element_type=f32)
 
     gather(2, mix_back)
     for j in range(n):
-        wide[j] = backs[j].T.astype(bf16)
+        wide[block(j), :] = backs[j].T.astype(bf16)
 
     @pl.loop(0, chunks)
     def _(c):
-        y[c] = (predict(c) - y[c].astype(f32)).astype(bf16)
+        spread = jnp.dot(phi[c], wide[...], preferred_element_type=f32)
+        y[c] = (spread + y[c].astype(f32)).astype(bf16)
         out_copy(c).start()
 
     for copy in started:
@@ -313,15 +357,15 @@
         functools.partial(kernel, n, nr),
         out_shape=(jax.ShapeDtypeStruct((rows, traits), bf16),
                    jax.ShapeDtypeStruct((1, width), f32)),
-        in_specs=[hbm, hbm, hbm, pl.BlockSpec(memory_space=pltpu.SMEM), vmem, vmem],
+        in_specs=[hbm] * 6,
         out_specs=(hbm, vmem),
         scratch_shapes=[
-            pltpu.VMEM((n, chunks, tall, width), bf16),
+            pltpu.VMEM((chunks, tall, n * width), bf16),
             pltpu.VMEM((chunks, tall, traits), bf16),
             pltpu.VMEM((chunks, traits, tall), bf16),
             pltpu.VMEM((n, width, width), bf16),
             pltpu.VMEM((n, n, width, width), bf16),
-            pltpu.VMEM((n, width, traits), bf16),
+            pltpu.VMEM((n * width, traits), bf16),
             pltpu.VMEM((2, n, traits, width), bf16),
             pltpu.VMEM((2, n, traits, width), bf16),
             pltpu.VMEM((3, n, traits, width), bf16),
@@ -329,13 +373,19 @@
             pltpu.VMEM((steps, 8, width), f32),
             pltpu.VMEM((2, steps, traits, width), bf16),
             pltpu.VMEM((2, steps, traits, width), bf16),
+            pltpu.SMEM(pattern.shape, jnp.int32),
+            pltpu.VMEM((1, width), f32),
+            pltpu.VMEM((1, width), f32),
+            pltpu.VMEM((n, traits, width), f32),
+            pltpu.VMEM((width, n * width), f32),
+            pltpu.VMEM((n, n, width, width), bf16),
             dma((n, chunks)), dma((chunks,)), dma((n,)), dma((chunks,)),
             dma((2, n)), dma((2, n)), dma((3, n)), dma((3, n)),
             dma((n, n)), dma((n, n)), dma((steps,)), dma((steps,)),
-            dma((2, steps)), dma((2, steps)),
+            dma((2, steps)), dma((2, steps)), dma((3,)),
         ],
         compiler_params=pltpu.CompilerParams(
-            collective_id=0, has_side_effects=True, vmem_limit_bytes=48 * 2**20),
+            collective_id=0, has_side_effects=True, vmem_limit_bytes=60 * 2**20),
         cost_estimate=pl.CostEstimate(
             flops=8 * rows * n * width * traits, transcendentals=0,
             bytes_accessed=2 * rows * (n * width + 2 * traits)),

time: 81.6 us -> 70.4 us (0.86)
  Pallas kernels: 74.1 us -> 66 us
  local copies, waits for them, and re-layouts: 6.55 us -> 3.61 us
    pallas_call x1, Pallas kernels: 74.1 us -> 66 us  [shards(): pl.pallas_call(functools.partial(kernel, n, nr), out_shape=(jax.ShapeDtyp...]
    unnamed x12 -> x4, local copies, waits for them, and re-layouts: 6.55 us -> 3.61 us
where the time goes in v2:
time: 70.4 us; the launch traced here: 70.2 us
  Pallas kernels  66 us (94%)
  local copies, waits for them, and re-layouts  3.61 us (5%)
    pallas_call x1, Pallas kernels, shards(): pl.pallas_call(functools.partial(kernel, n, nr), out_shape=(jax.ShapeDtyp...  66 us
    unnamed x4, local copies, waits for them, and re-layouts  3.61 us

profile of v2, /device:TPU:1, one launch (start us, length us, event | category | flops | bytes accessed | tf_op | source)
XLA Modules:
  0.0 70.2 jit_solution(5798030759061685571)
XLA Ops:
  0.6 66.0 %shard_map.77 = (bf16[8192,128]{1,0:T(8,128)(2,1)}, f32[1,256]{1,0:T(1,128)}) custom-call(bf16[8192,128]{1,0:T(8,128)(2,1)} %y_hbm.1, bf16[8192,1024]{1,0:T(8,128)(2,1)} %phi_hbm.1, bf16[256,1024]{1,0:T(8,128)(2,1)} %mix_hbm.1, s32[8,8]{1,0:T(8,128)} %pattern_hbm.1, f32[1,256]{1,0:T(1,128)} %decays_hbm.1, f32[1,256]{1,0:T(1,128)} %bitcast.1), custom_call_target="tpu_custom_call" | custom-call | flops 8589934592 | bytes 20971520 | tf_op jit(solution)/shard_map/pallas_call | solution.py:356
  66.6 0.0 copy-start
  66.6 3.0 %copy.10 = bf16[8192,128]{1,0:T(8,128)(2,1)} copy(bf16[8192,128]{1,0:T(8,128)(2,1)} %get-tuple-element.4) | data formatting | bytes 4194304
  69.7 0.0 copy-done
  69.7 0.6 copy.11
Async XLA Ops:
  66.6 3.1 %copy-start = (f32[1,256]{1,0:T(1,128)S(1)}, f32[1,256]{1,0:T(1,128)}, u32[]{:S(2)}) copy-start(f32[1,256]{1,0:T(1,128)} %get-tuple-element.5) | copy-start | bytes 3076

commit v3 on v2

--- a/solution.py
+++ b/solution.py
@@ -171,6 +171,11 @@
         rates["after"] = jnp.where(up, after, theirs * after)
         rates["own"] = own * theirs
 
+    def rate_step(k):
+        rate_end(k)
+        if k + 1 < steps:
+            rate_start(k + 1)
+
     def scan(use, total, work=lambda: None):
         carried = jnp.zeros_like(total)
         for k in range(steps):
@@ -230,10 +235,7 @@
                     send_part(0, m, parts[m])
             if first:
                 build_mixer()
-            for k in range(0 if first else 1, 1 if first else steps):
-                rate_end(k)
-                if k + 1 < steps:
-                    rate_start(k + 1)
+                rate_step(0)
 
     def gram_piece(m, start, stop):
         span = block(m, n - m)
@@ -256,18 +258,32 @@
                         gram[other, m] = found.T.astype(bf16)
         return piece
 
-    cuts = {0: (0, 3, 6, chunks), 1: (0, 4, chunks)}
-    pieces = []
-    for m in range(n):
-        cut = cuts.get(m, (0, chunks))
-        pieces += [gram_piece(m, *ends) for ends in zip(cut[:-1], cut[1:])]
+    shares = [1.0, 3.0, 1.0] + [3.75] * (steps - 1) + [5.0, 2.5]
+    units = [(m, c) for m in range(n) for c in range(chunks)]
+    cost = sum(n - m for m, _ in units) / sum(shares)
+    slots, spent, limit = [], 0.0, 0.0
+    for share in shares:
+        limit += share * cost
+        taken = []
+        while units and spent + 0.5 < limit:
+            m, c = units.pop(0)
+            spent += n - m
+            if taken and taken[-1][0] == m:
+                taken[-1][2] = c + 1
+            else:
+                taken.append([m, c, c + 1])
+        slots.append(taken)
+    slots[-1] += [[m, c, c + 1] for m, c in units]
 
     def work():
-        if pieces:
-            pieces.pop(0)()
+        if slots:
+            for m, start, stop in slots.pop(0):
+                gram_piece(m, start, stop)()
 
     rate_start(0)
     project()
+    if steps > 1:
+        rate_step(1)
     work()
     gathered[0, 0] = owned(0, parts[0]).astype(bf16)
     sums = []
@@ -277,6 +293,8 @@
                                     preferred_element_type=f32))
 
     gather(0, mix_in, work)
+    for k in range(2, steps):
+        rate_step(k)
     mixed = functools.reduce(jnp.add, sums)
 
     plan = fan_order(n)
@@ -289,7 +307,7 @@
     state = rate * previous + mixed
     gathered[1, 0] = (load * state).astype(bf16)
     gather(1, lambda m: None, work)
-    while pieces:
+    while slots:
         work()
 
     for m in order:
@@ -385,7 +403,7 @@
             dma((2, steps)), dma((2, steps)), dma((3,)),
         ],
         compiler_params=pltpu.CompilerParams(
-            collective_id=0, has_side_effects=True, vmem_limit_bytes=60 * 2**20),
+            collective_id=0, has_side_effects=True, vmem_limit_bytes=57 * 2**20),
         cost_estimate=pl.CostEstimate(
             flops=8 * rows * n * width * traits, transcendentals=0,
             bytes_accessed=2 * rows * (n * width + 2 * traits)),

time: 70.4 us -> 67.8 us (0.963)
  Pallas kernels: 66 us -> 63.4 us
    pallas_call x1, Pallas kernels: 66 us -> 63.4 us  [shards(): pl.pallas_call(functools.partial(kernel, n, nr), out_shape=(jax.ShapeDtyp...]
where the time goes in v3:
time: 67.8 us; the launch traced here: 67.6 us
  Pallas kernels  63.4 us (94%)
  local copies, waits for them, and re-layouts  3.61 us (5%)
    pallas_call x1, Pallas kernels, shards(): pl.pallas_call(functools.partial(kernel, n, nr), out_shape=(jax.ShapeDtyp...  63.4 us
    unnamed x4, local copies, waits for them, and re-layouts  3.61 us

profile of v3, /device:TPU:1, one launch (start us, length us, event | category | flops | bytes accessed | tf_op | source)
XLA Modules:
  0.0 67.6 jit_solution(10418108341771574468)
XLA Ops:
  0.6 63.4 %shard_map.77 = (bf16[8192,128]{1,0:T(8,128)(2,1)}, f32[1,256]{1,0:T(1,128)}) custom-call(bf16[8192,128]{1,0:T(8,128)(2,1)} %y_hbm.1, bf16[8192,1024]{1,0:T(8,128)(2,1)} %phi_hbm.1, bf16[256,1024]{1,0:T(8,128)(2,1)} %mix_hbm.1, s32[8,8]{1,0:T(8,128)} %pattern_hbm.1, f32[1,256]{1,0:T(1,128)} %decays_hbm.1, f32[1,256]{1,0:T(1,128)} %bitcast.1), custom_call_target="tpu_custom_call" | custom-call | flops 8589934592 | bytes 20971520 | tf_op jit(solution)/shard_map/pallas_call | solution.py:374
  64.0 0.0 copy-start
  64.0 3.0 %copy.10 = bf16[8192,128]{1,0:T(8,128)(2,1)} copy(bf16[8192,128]{1,0:T(8,128)(2,1)} %get-tuple-element.4) | data formatting | bytes 4194304
  67.1 0.0 copy-done
  67.1 0.6 copy.11
Async XLA Ops:
  64.0 3.1 %copy-start = (f32[1,256]{1,0:T(1,128)S(1)}, f32[1,256]{1,0:T(1,128)}, u32[]{:S(2)}) copy-start(f32[1,256]{1,0:T(1,128)} %get-tuple-element.5) | copy-start | bytes 3076

commit v4 on v3

--- a/solution.py
+++ b/solution.py
@@ -9,6 +9,7 @@
 
 BLOCK = 128
 CHUNKS = 8
+SPLIT = 2
 MESH = pl.DeviceIdType.MESH
 
 
@@ -40,6 +41,11 @@
     across = [flip(r, 1 << k, nr) for k in range(steps)]
     order = list(range(n - 1, -1, -1))
     half = n // 2
+    tall_part = traits // SPLIT
+    splits = range(SPLIT)
+
+    def rows(h):
+        return pl.ds(h * tall_part, tall_part)
 
     def block(m, count=1):
         return pl.ds(m * width, count * width)
@@ -102,31 +108,38 @@
             src_ref=src, dst_ref=dst, send_sem=send_sem, recv_sem=recv_sem,
             device_id={"region": across[k]}, device_id_type=MESH)
 
-    def gather_copy(use, m):
+    plan = fan_order(n)
+    direct = [m for m in plan if bin(m).count("1") == 1]
+
+    def gather_copy(use, m, h):
         low = m & -m
-        return to_mate(gathered.at[use, m ^ low], gathered.at[use, m],
-                       ag_send.at[use, m], ag_recv.at[use, m], low)
-
-    def gather(use, consume, work=lambda: None):
+        return to_mate(gathered.at[use, m ^ low, rows(h)], gathered.at[use, m, rows(h)],
+                       ag_send.at[use, m, h], ag_recv.at[use, m, h], low)
+
+    def gather_start(use, h, value):
+        gathered[use, 0, rows(h)] = value.astype(bf16)
+        for m in direct:
+            send(gather_copy(use, m, h))
+
+    def gather_finish(use, consume, work=lambda: None):
         ready = {0}
-        plan = fan_order(n)
-        for m in plan:
-            if bin(m).count("1") == 1:
-                send(gather_copy(use, m))
         consume(0)
         for m in plan:
             source = m ^ (m & -m)
-            if bin(m).count("1") > 1:
+            if m not in direct:
                 if source not in ready:
                     work()
-                    gather_copy(use, source).wait_recv()
-                    ready.add(source)
-                send(gather_copy(use, m))
+                for h in splits:
+                    if source not in ready:
+                        gather_copy(use, source, h).wait_recv()
+                    send(gather_copy(use, m, h))
+                ready.add(source)
         for m in range(1, n):
             if m not in ready:
                 if m == n - 1:
                     work()
-                gather_copy(use, m).wait_recv()
+                for h in splits:
+                    gather_copy(use, m, h).wait_recv()
                 ready.add(m)
             consume(m)
 
@@ -135,16 +148,16 @@
         return to_mate(mixer.at[m ^ low, j ^ low], mixer.at[m, j],
                        mx_send.at[m, j], mx_recv.at[m, j], low)
 
-    def part_copy(use, m):
-        return to_mate(rs_src.at[use, m], rs_dst.at[use, m],
-                       rs_send.at[use, m], rs_recv.at[use, m], m)
+    def part_copy(use, m, h):
+        return to_mate(rs_src.at[use, m, rows(h)], rs_dst.at[use, m, rows(h)],
+                       rs_send.at[use, m, h], rs_recv.at[use, m, h], m)
 
     def rate_copy(k):
         return to_across(a_src.at[k], a_dst.at[k], a_send.at[k], a_recv.at[k], k)
 
-    def scan_copy(use, k):
-        return to_across(s_src.at[use, k], s_dst.at[use, k],
-                         s_send.at[use, k], s_recv.at[use, k], k)
+    def scan_copy(use, k, h):
+        return to_across(s_src.at[use, k, rows(h)], s_dst.at[use, k, rows(h)],
+                         s_send.at[use, k, h], s_recv.at[use, k, h], k)
 
     for copy in small:
         copy.wait()
@@ -176,18 +189,33 @@
         if k + 1 < steps:
             rate_start(k + 1)
 
-    def scan(use, total, work=lambda: None):
-        carried = jnp.zeros_like(total)
+    def scan(use, total_of, finish, work):
+        totals, carried = [], []
+
+        def leave(k, h):
+            s_src[use, k, rows(h)] = totals[h].astype(bf16)
+            send(scan_copy(use, k, h))
+
+        for h in splits:
+            totals.append(total_of(h))
+            carried.append(jnp.zeros_like(totals[h]))
+            if steps:
+                leave(0, h)
         for k in range(steps):
-            s_src[use, k] = total.astype(bf16)
-            send(scan_copy(use, k))
             keep, take, enter = factors[k][use]
             work()
-            scan_copy(use, k).wait_recv()
-            other = s_dst[use, k].astype(f32)
-            carried = carried + enter * other
-            total = keep * total + take * other
-        return carried
+            for h in splits:
+                scan_copy(use, k, h).wait_recv()
+                other = s_dst[use, k, rows(h)].astype(f32)
+                carried[h] = carried[h] + enter * other
+                totals[h] = keep * totals[h] + take * other
+                if k + 1 < steps:
+                    leave(k + 1, h)
+                else:
+                    finish(h, carried[h])
+        if not steps:
+            for h in splits:
+                finish(h, carried[h])
 
     def build_mixer():
         rows = lax.broadcasted_iota(jnp.int32, (BLOCK, BLOCK), 0)
@@ -207,14 +235,14 @@
     def turned(block):
         return block.astype(f32).T.astype(bf16)
 
-    def send_part(use, m, value):
-        rs_src[use, m] = value.astype(bf16)
-        send(part_copy(use, m))
-
-    def owned(use, total):
+    def send_part(use, m, h):
+        send(part_copy(use, m, h))
+
+    def owned(use, own, h):
+        total = own
         for m in order[:-1]:
-            part_copy(use, m).wait_recv()
-            total = total + rs_dst[use, m].astype(f32)
+            part_copy(use, m, h).wait_recv()
+            total = total + rs_dst[use, m, rows(h)].astype(f32)
         return total
 
     def project():
@@ -232,7 +260,9 @@
             for m in reversed(range(first, first + half)):
                 parts[m] = total[:, (m - first) * width:(m - first + 1) * width]
                 if m:
-                    send_part(0, m, parts[m])
+                    rs_src[0, m] = parts[m].astype(bf16)
+                    for h in splits:
+                        send_part(0, m, h)
             if first:
                 build_mixer()
                 rate_step(0)
@@ -285,45 +315,74 @@
     if steps > 1:
         rate_step(1)
     work()
-    gathered[0, 0] = owned(0, parts[0]).astype(bf16)
+    for h in splits:
+        gather_start(0, h, owned(0, parts[0, rows(h)], h))
     sums = []
 
     def mix_in(m):
         sums.append(lax.dot_general(gathered[0, m], mixer[0, m], (((1,), (1,)), ((), ())),
                                     preferred_element_type=f32))
 
-    gather(0, mix_in, work)
+    gather_finish(0, mix_in, work)
     for k in range(2, steps):
         rate_step(k)
     mixed = functools.reduce(jnp.add, sums)
 
-    plan = fan_order(n)
-    direct = [m for m in plan if bin(m).count("1") == 1]
-    for m in direct:
-        for j in range(half):
-            send(mixer_copy(m, j))
-
-    previous = scan(0, mixed, work)
-    state = rate * previous + mixed
-    gathered[1, 0] = (load * state).astype(bf16)
-    gather(1, lambda m: None, work)
-    while slots:
+    def part_of(value, h):
+        return value[h * tall_part:(h + 1) * tall_part]
+
+    mixer_shares = [(m, j) for j in range(n) for m in direct]
+
+    def spread_mixer(count):
+        for _ in range(min(count, len(mixer_shares))):
+            send(mixer_copy(*mixer_shares.pop(0)))
+
+    previous = {}
+
+    def enter(h, carried):
+        previous[h] = carried
+        gather_start(1, h, load * (rate * carried + part_of(mixed, h)))
+
+    def forward_work():
+        if len(mixer_shares) == n * len(direct):
+            spread_mixer(half * len(direct))
         work()
 
-    for m in order:
-        pull = -parts[m]
-        for other in range(n):
-            pull = pull + jnp.dot(gathered[1, other], gram[other, m], preferred_element_type=f32)
-        if m:
-            send_part(1, m, pull)
-    pulled = load * owned(1, pull)
-
-    for m in direct:
-        for j in range(half, n):
-            send(mixer_copy(m, j))
-    adjoint = pulled + scan(1, rate * pulled)
-    gathered[2, 0] = adjoint.astype(bf16)
-    slope[...] = jnp.sum(adjoint * previous, axis=0, keepdims=True) / traits
+    scan(0, lambda h: part_of(mixed, h), enter, forward_work)
+    pulls = [-parts[m] for m in range(n)]
+
+    def all_pulls():
+        while slots:
+            work()
+        for m in order:
+            for source in range(n):
+                pulls[m] = pulls[m] + jnp.dot(gathered[1, source], gram[source, m],
+                                              preferred_element_type=f32)
+            if m:
+                rs_src[1, m] = pulls[m].astype(bf16)
+                send_part(1, m, 0)
+        for h in splits[1:]:
+            for m in order[:-1]:
+                send_part(1, m, h)
+
+    gather_finish(1, lambda m: None, work)
+    all_pulls()
+    pulled = {}
+
+    def pulled_of(h):
+        pulled[h] = load * owned(1, part_of(pulls[0], h), h)
+        return rate * pulled[h]
+
+    slopes = []
+
+    def leave(h, carried):
+        adjoint = pulled[h] + carried
+        gather_start(2, h, adjoint)
+        slopes.append(jnp.sum(adjoint * previous[h], axis=0, keepdims=True))
+
+    scan(1, pulled_of, leave, lambda: spread_mixer(n * len(direct)))
+    spread_mixer(n * len(direct))
+    slope[...] = functools.reduce(jnp.add, slopes) / traits
     backs = [-gathered[1, j].astype(f32) for j in range(n)]
     seen = set()
 
@@ -344,7 +403,7 @@
         for j in range(n):
             backs[j] = backs[j] + jnp.dot(gathered[2, m], mixer[m, j], preferred_element_type=f32)
 
-    gather(2, mix_back)
+    gather_finish(2, mix_back)
     for j in range(n):
         wide[block(j), :] = backs[j].T.astype(bf16)
 
@@ -398,9 +457,9 @@
             pltpu.VMEM((width, n * width), f32),
             pltpu.VMEM((n, n, width, width), bf16),
             dma((n, chunks)), dma((chunks,)), dma((n,)), dma((chunks,)),
-            dma((2, n)), dma((2, n)), dma((3, n)), dma((3, n)),
+            dma((2, n, SPLIT)), dma((2, n, SPLIT)), dma((3, n, SPLIT)), dma((3, n, SPLIT)),
             dma((n, n)), dma((n, n)), dma((steps,)), dma((steps,)),
-            dma((2, steps)), dma((2, steps)), dma((3,)),
+            dma((2, steps, SPLIT)), dma((2, steps, SPLIT)), dma((3,)),
         ],
         compiler_params=pltpu.CompilerParams(
             collective_id=0, has_side_effects=True, vmem_limit_bytes=57 * 2**20),

time: 67.8 us -> 65.9 us (0.972)
  Pallas kernels: 63.4 us -> 61.5 us
    pallas_call x1, Pallas kernels: 63.4 us -> 61.5 us  [shards(): pl.pallas_call(functools.partial(kernel, n, nr), out_shape=(jax.ShapeDtyp...]
where the time goes in v4:
time: 65.9 us; the launch traced here: 65.8 us
  Pallas kernels  61.5 us (93%)
  local copies, waits for them, and re-layouts  3.61 us (5%)
    pallas_call x1, Pallas kernels, shards(): pl.pallas_call(functools.partial(kernel, n, nr), out_shape=(jax.ShapeDtyp...  61.5 us
    unnamed x4, local copies, waits for them, and re-layouts  3.61 us

profile of v4, /device:TPU:1, one launch (start us, length us, event | category | flops | bytes accessed | tf_op | source)
XLA Modules:
  0.0 65.8 jit_solution(12934290720506951779)
XLA Ops:
  0.6 61.5 %shard_map.77 = (bf16[8192,128]{1,0:T(8,128)(2,1)}, f32[1,256]{1,0:T(1,128)}) custom-call(bf16[8192,128]{1,0:T(8,128)(2,1)} %y_hbm.1, bf16[8192,1024]{1,0:T(8,128)(2,1)} %phi_hbm.1, bf16[256,1024]{1,0:T(8,128)(2,1)} %mix_hbm.1, s32[8,8]{1,0:T(8,128)} %pattern_hbm.1, f32[1,256]{1,0:T(1,128)} %decays_hbm.1, f32[1,256]{1,0:T(1,128)} %bitcast.1), custom_call_target="tpu_custom_call" | custom-call | flops 8589934592 | bytes 20971520 | tf_op jit(solution)/shard_map/pallas_call | solution.py:433
  62.2 0.0 copy-start
  62.2 3.0 %copy.10 = bf16[8192,128]{1,0:T(8,128)(2,1)} copy(bf16[8192,128]{1,0:T(8,128)(2,1)} %get-tuple-element.4) | data formatting | bytes 4194304
  65.2 0.0 copy-done
  65.2 0.6 copy.11
Async XLA Ops:
  62.2 3.1 %copy-start = (f32[1,256]{1,0:T(1,128)S(1)}, f32[1,256]{1,0:T(1,128)}, u32[]{:S(2)}) copy-start(f32[1,256]{1,0:T(1,128)} %get-tuple-element.5) | copy-start | bytes 3076

commit v5 on v4

--- a/solution.py
+++ b/solution.py
@@ -27,7 +27,7 @@
 
 def kernel(n, nr, y_hbm, phi_hbm, mix_hbm, pattern_hbm, decays_hbm, loadings_hbm, out_hbm, slope,
            phi, y, yt, mixraw, mixer, wide, rs_src, rs_dst, gathered, a_src, a_dst, s_src, s_dst,
-           pattern, decays, loadings, parts, gram_row, gram,
+           pattern, decays, loadings, parts, gram_row, gram_high, gram,
            phi_sem, y_sem, mix_sem, out_sem, rs_send, rs_recv, ag_send, ag_recv,
            mx_send, mx_recv, a_send, a_recv, s_send, s_recv, small_sem):
     b, r = lax.axis_index("basis"), lax.axis_index("region")
@@ -245,9 +245,25 @@
             total = total + rs_dst[use, m, rows(h)].astype(f32)
         return total
 
+    def cross(c, m):
+        return lax.dot_general(phi[c, :, block(m)], phi[c, :, block(m, n - m)],
+                               (((0,), (0,)), ((), ())), preferred_element_type=f32)
+
+    def keep_gram(m, other, found):
+        gram[m, other] = found.astype(bf16)
+        if other != m:
+            gram[other, m] = found.T.astype(bf16)
+
     def project():
         for first in (half, 0):
+            if not first:
+                gram_high[...] = jnp.zeros_like(gram_high)
+
             def body(c, total):
+                if not first:
+                    for m in range(half, n):
+                        span = pl.ds((m - half) * width, (n - m) * width)
+                        gram_high[m - half, :, span] += cross(c, m)
                 if first:
                     y_copy(c).wait()
                     yt[c] = turned(y[c])
@@ -276,20 +292,15 @@
 
             @pl.loop(start, stop)
             def _(c):
-                gram_row[:, span] += lax.dot_general(
-                    phi[c, :, block(m)], phi[c, :, span], (((0,), (0,)), ((), ())),
-                    preferred_element_type=f32)
+                gram_row[:, span] += cross(c, m)
 
             if stop == chunks:
                 for other in range(m, n):
-                    found = gram_row[:, block(other)]
-                    gram[m, other] = found.astype(bf16)
-                    if other != m:
-                        gram[other, m] = found.T.astype(bf16)
+                    keep_gram(m, other, gram_row[:, block(other)])
         return piece
 
-    shares = [1.0, 3.0, 1.0] + [3.75] * (steps - 1) + [5.0, 2.5]
-    units = [(m, c) for m in range(n) for c in range(chunks)]
+    shares = [0.0, 3.0, 0.7] + [3.75] * (steps - 1) + [5.0, 2.5]
+    units = [(m, c) for m in range(half) for c in range(chunks)]
     cost = sum(n - m for m, _ in units) / sum(shares)
     slots, spent, limit = [], 0.0, 0.0
     for share in shares:
@@ -314,6 +325,9 @@
     project()
     if steps > 1:
         rate_step(1)
+    for m in range(half, n):
+        for other in range(m, n):
+            keep_gram(m, other, gram_high[m - half, :, block(other - half)])
     work()
     for h in splits:
         gather_start(0, h, owned(0, parts[0, rows(h)], h))
@@ -351,22 +365,20 @@
     scan(0, lambda h: part_of(mixed, h), enter, forward_work)
     pulls = [-parts[m] for m in range(n)]
 
-    def all_pulls():
-        while slots:
-            work()
+    def pull_in(source):
         for m in order:
-            for source in range(n):
-                pulls[m] = pulls[m] + jnp.dot(gathered[1, source], gram[source, m],
-                                              preferred_element_type=f32)
-            if m:
+            pulls[m] = pulls[m] + jnp.dot(gathered[1, source], gram[source, m],
+                                          preferred_element_type=f32)
+            if m and source == n - 1:
                 rs_src[1, m] = pulls[m].astype(bf16)
                 send_part(1, m, 0)
-        for h in splits[1:]:
-            for m in order[:-1]:
-                send_part(1, m, h)
-
-    gather_finish(1, lambda m: None, work)
-    all_pulls()
+
+    while slots:
+        work()
+    gather_finish(1, pull_in)
+    for h in splits[1:]:
+        for m in order[:-1]:
+            send_part(1, m, h)
     pulled = {}
 
     def pulled_of(h):
@@ -455,6 +467,7 @@
             pltpu.VMEM((1, width), f32),
             pltpu.VMEM((n, traits, width), f32),
             pltpu.VMEM((width, n * width), f32),
+            pltpu.VMEM((n - n // 2, width, (n - n // 2) * width), f32),
             pltpu.VMEM((n, n, width, width), bf16),
             dma((n, chunks)), dma((chunks,)), dma((n,)), dma((chunks,)),
             dma((2, n, SPLIT)), dma((2, n, SPLIT)), dma((3, n, SPLIT)), dma((3, n, SPLIT)),

time: 65.9 us -> 69.6 us (1.056)
  Pallas kernels: 61.5 us -> 65.1 us
    pallas_call x1, Pallas kernels: 61.5 us -> 65.1 us  [shards(): pl.pallas_call(functools.partial(kernel, n, nr), out_shape=(jax.ShapeDtyp...]
where the time goes in v5:
time: 69.6 us; the launch traced here: 69.4 us
  Pallas kernels  65.1 us (94%)
  local copies, waits for them, and re-layouts  3.61 us (5%)
    pallas_call x1, Pallas kernels, shards(): pl.pallas_call(functools.partial(kernel, n, nr), out_shape=(jax.ShapeDtyp...  65.1 us
    unnamed x4, local copies, waits for them, and re-layouts  3.61 us

profile of v5, /device:TPU:1, one launch (start us, length us, event | category | flops | bytes accessed | tf_op | source)
XLA Modules:
  0.0 69.4 jit_solution(3866202448326072702)
XLA Ops:
  0.6 65.1 %shard_map.77 = (bf16[8192,128]{1,0:T(8,128)(2,1)}, f32[1,256]{1,0:T(1,128)}) custom-call(bf16[8192,128]{1,0:T(8,128)(2,1)} %y_hbm.1, bf16[8192,1024]{1,0:T(8,128)(2,1)} %phi_hbm.1, bf16[256,1024]{1,0:T(8,128)(2,1)} %mix_hbm.1, s32[8,8]{1,0:T(8,128)} %pattern_hbm.1, f32[1,256]{1,0:T(1,128)} %decays_hbm.1, f32[1,256]{1,0:T(1,128)} %bitcast.1), custom_call_target="tpu_custom_call" | custom-call | flops 8589934592 | bytes 20971520 | tf_op jit(solution)/shard_map/pallas_call | solution.py:445
  65.8 0.0 copy-start
  65.8 3.0 %copy.10 = bf16[8192,128]{1,0:T(8,128)(2,1)} copy(bf16[8192,128]{1,0:T(8,128)(2,1)} %get-tuple-element.4) | data formatting | bytes 4194304
  68.8 0.0 copy-done
  68.8 0.6 copy.11
Async XLA Ops:
  65.8 3.1 %copy-start = (f32[1,256]{1,0:T(1,128)S(1)}, f32[1,256]{1,0:T(1,128)}, u32[]{:S(2)}) copy-start(f32[1,256]{1,0:T(1,128)} %get-tuple-element.5) | copy-start | bytes 3076

commit v6 on v4

--- a/solution.py
+++ b/solution.py
@@ -351,22 +351,20 @@
     scan(0, lambda h: part_of(mixed, h), enter, forward_work)
     pulls = [-parts[m] for m in range(n)]
 
-    def all_pulls():
-        while slots:
-            work()
+    def pull_in(source):
         for m in order:
-            for source in range(n):
-                pulls[m] = pulls[m] + jnp.dot(gathered[1, source], gram[source, m],
-                                              preferred_element_type=f32)
-            if m:
+            pulls[m] = pulls[m] + jnp.dot(gathered[1, source], gram[source, m],
+                                          preferred_element_type=f32)
+            if m and source == n - 1:
                 rs_src[1, m] = pulls[m].astype(bf16)
                 send_part(1, m, 0)
-        for h in splits[1:]:
-            for m in order[:-1]:
-                send_part(1, m, h)
-
-    gather_finish(1, lambda m: None, work)
-    all_pulls()
+
+    while slots:
+        work()
+    gather_finish(1, pull_in)
+    for h in splits[1:]:
+        for m in order[:-1]:
+            send_part(1, m, h)
     pulled = {}
 
     def pulled_of(h):
@@ -405,12 +403,13 @@
 
     gather_finish(2, mix_back)
     for j in range(n):
-        wide[block(j), :] = backs[j].T.astype(bf16)
+        wide[:, block(j)] = backs[j].astype(bf16)
 
     @pl.loop(0, chunks)
     def _(c):
-        spread = jnp.dot(phi[c], wide[...], preferred_element_type=f32)
-        y[c] = (spread + y[c].astype(f32)).astype(bf16)
+        spread = lax.dot_general(wide[...], phi[c], (((1,), (1,)), ((), ())),
+                                 preferred_element_type=f32)
+        y[c] = spread.T.astype(bf16)
         out_copy(c).start()
 
     for copy in started:
@@ -430,7 +429,7 @@
     dma = pltpu.SemaphoreType.DMA
     hbm = pl.BlockSpec(memory_space=pl.ANY)
     vmem = pl.BlockSpec(memory_space=pltpu.VMEM)
-    return pl.pallas_call(
+    spread, slope = pl.pallas_call(
         functools.partial(kernel, n, nr),
         out_shape=(jax.ShapeDtypeStruct((rows, traits), bf16),
                    jax.ShapeDtypeStruct((1, width), f32)),
@@ -442,7 +441,7 @@
             pltpu.VMEM((chunks, traits, tall), bf16),
             pltpu.VMEM((n, width, width), bf16),
             pltpu.VMEM((n, n, width, width), bf16),
-            pltpu.VMEM((n * width, traits), bf16),
+            pltpu.VMEM((traits, n * width), bf16),
             pltpu.VMEM((2, n, traits, width), bf16),
             pltpu.VMEM((2, n, traits, width), bf16),
             pltpu.VMEM((3, n, traits, width), bf16),
@@ -467,6 +466,7 @@
             flops=8 * rows * n * width * traits, transcendentals=0,
             bytes_accessed=2 * rows * (n * width + 2 * traits)),
     )(observations, basis_values, mixing, pattern, decays, loadings.reshape(1, width))
+    return (spread.astype(f32) + observations.astype(f32)).astype(bf16), slope
 
 
 def solution(mesh):

time: 65.9 us -> 67.7 us (1.027)
  other arithmetic: 0 us -> 3.45 us
  local copies, waits for them, and re-layouts: 3.61 us -> 0.57 us
  Pallas kernels: 61.5 us -> 62.9 us
    convert_element_type x0 -> x1, other arithmetic: none -> 3.45 us  [shards(): return ((spread.astype(f32) + observations.astype(f32)).astype(bf16), slope)]
    unnamed x4 -> x5, local copies, waits for them, and re-layouts: 3.61 us -> 0.57 us
    pallas_call x1, Pallas kernels: 61.5 us -> 62.9 us  [shards(): pl.pallas_call(functools.partial(kernel, n, nr), out_shape=(jax.ShapeDtyp...]
where the time goes in v6:
time: 67.7 us; the launch traced here: 67.5 us
  Pallas kernels  62.9 us (93%)
  other arithmetic  3.45 us (5%)
    pallas_call x1, Pallas kernels, shards(): pl.pallas_call(functools.partial(kernel, n, nr), out_shape=(jax.ShapeDtyp...  62.9 us
    convert_element_type x1, other arithmetic, shards(): return ((spread.astype(f32) + observations.astype(f32)).astype(bf16), slope)  3.45 us

profile of v6, /device:TPU:1, one launch (start us, length us, event | category | flops | bytes accessed | tf_op | source)
XLA Modules:
  0.0 67.5 jit_solution(10906006608243401)
XLA Ops:
  0.6 0.0 copy-start
  0.6 62.9 %shard_map.77 = (bf16[8192,128]{1,0:T(8,128)(2,1)}, f32[1,256]{1,0:T(1,128)}) custom-call(bf16[8192,128]{1,0:T(8,128)(2,1)} %y_hbm.1, bf16[8192,1024]{1,0:T(8,128)(2,1)} %phi_hbm.1, bf16[256,1024]{1,0:T(8,128)(2,1)} %mix_hbm.1, s32[8,8]{1,0:T(8,128)} %pattern_hbm.1, f32[1,256]{1,0:T(1,128)} %decays_hbm.1, f32[1,256]{1,0:T(1,128)} %bitcast.1), custom_call_target="tpu_custom_call" | custom-call | flops 8589934592 | bytes 20971520 | tf_op jit(solution)/shard_map/pallas_call | solution.py:432
  63.5 0.0 copy-done
  63.5 0.0 copy-start.1
  63.5 3.5 %add_convert_fusion = bf16[8192,128]{1,0:T(8,128)(2,1)} fusion(bf16[8192,128]{1,0:T(8,128)(2,1)S(1)} %copy-done, bf16[8192,128]{1,0:T(8,128)(2,1)} %get-tuple-element.4), kind=kLoop, calls=%fused_computation | loop fusion | flops 4194304 | bytes 6291456 | tf_op jit(solution)/shard_map/convert_element_type | solution.py:469
  67.0 0.0 copy-done.1
  67.0 0.6 copy.9
Async XLA Ops:
  0.6 62.9 %copy-start = (bf16[8192,128]{1,0:T(8,128)(2,1)S(1)}, bf16[8192,128]{1,0:T(8,128)(2,1)}, u32[]{:S(2)}) copy-start(bf16[8192,128]{1,0:T(8,128)(2,1)} %y_hbm.1) | copy-start | bytes 6291460
  63.5 3.5 %copy-start.1 = (f32[1,256]{1,0:T(1,128)S(1)}, f32[1,256]{1,0:T(1,128)}, u32[]{:S(2)}) copy-start(f32[1,256]{1,0:T(1,128)} %get-tuple-element.9) | copy-start | bytes 3076

commit v7 on v6

--- a/solution.py
+++ b/solution.py
@@ -10,6 +10,7 @@
 BLOCK = 128
 CHUNKS = 8
 SPLIT = 2
+TOGETHER = 2
 MESH = pl.DeviceIdType.MESH
 
 
@@ -403,14 +404,16 @@
 
     gather_finish(2, mix_back)
     for j in range(n):
-        wide[:, block(j)] = backs[j].astype(bf16)
-
-    @pl.loop(0, chunks)
-    def _(c):
-        spread = lax.dot_general(wide[...], phi[c], (((1,), (1,)), ((), ())),
-                                 preferred_element_type=f32)
-        y[c] = spread.T.astype(bf16)
-        out_copy(c).start()
+        wide[block(j), :] = backs[j].T.astype(bf16)
+
+    @pl.loop(0, chunks // TOGETHER)
+    def _(turn):
+        for at in range(TOGETHER):
+            c = turn * TOGETHER + at
+            spread = jnp.dot(phi[c], wide[...], preferred_element_type=f32)
+            y[c] = (spread + y[c].astype(f32)).astype(bf16)
+        for at in range(TOGETHER):
+            out_copy(turn * TOGETHER + at).start()
 
     for copy in started:
         copy.wait_send()
@@ -429,7 +432,7 @@
     dma = pltpu.SemaphoreType.DMA
     hbm = pl.BlockSpec(memory_space=pl.ANY)
     vmem = pl.BlockSpec(memory_space=pltpu.VMEM)
-    spread, slope = pl.pallas_call(
+    return pl.pallas_call(
         functools.partial(kernel, n, nr),
         out_shape=(jax.ShapeDtypeStruct((rows, traits), bf16),
                    jax.ShapeDtypeStruct((1, width), f32)),
@@ -441,7 +444,7 @@
             pltpu.VMEM((chunks, traits, tall), bf16),
             pltpu.VMEM((n, width, width), bf16),
             pltpu.VMEM((n, n, width, width), bf16),
-            pltpu.VMEM((traits, n * width), bf16),
+            pltpu.VMEM((n * width, traits), bf16),
             pltpu.VMEM((2, n, traits, width), bf16),
             pltpu.VMEM((2, n, traits, width), bf16),
             pltpu.VMEM((3, n, traits, width), bf16),
@@ -466,7 +469,6 @@
             flops=8 * rows * n * width * traits, transcendentals=0,
             bytes_accessed=2 * rows * (n * width + 2 * traits)),
     )(observations, basis_values, mixing, pattern, decays, loadings.reshape(1, width))
-    return (spread.astype(f32) + observations.astype(f32)).astype(bf16), slope
 
 
 def solution(mesh):

time: 67.7 us -> 65.4 us (0.966)
  other arithmetic: 3.45 us -> 0 us
  local copies, waits for them, and re-layouts: 0.57 us -> 3.61 us
  Pallas kernels: 62.9 us -> 61 us
    convert_element_type x1 -> x0, other arithmetic: 3.45 us -> none  [shards(): return ((spread.astype(f32) + observations.astype(f32)).astype(bf16), slope)]
    unnamed x5 -> x4, local copies, waits for them, and re-layouts: 0.57 us -> 3.61 us
    pallas_call x1, Pallas kernels: 62.9 us -> 61 us  [shards(): pl.pallas_call(functools.partial(kernel, n, nr), out_shape=(jax.ShapeDtyp...]
where the time goes in v7:
time: 65.4 us; the launch traced here: 65.2 us
  Pallas kernels  61 us (93%)
  local copies, waits for them, and re-layouts  3.61 us (6%)
    pallas_call x1, Pallas kernels, shards(): pl.pallas_call(functools.partial(kernel, n, nr), out_shape=(jax.ShapeDtyp...  61 us
    unnamed x4, local copies, waits for them, and re-layouts  3.61 us

profile of v7, /device:TPU:1, one launch (start us, length us, event | category | flops | bytes accessed | tf_op | source)
XLA Modules:
  0.0 65.2 jit_solution(13127578447362419338)
XLA Ops:
  0.6 61.0 %shard_map.77 = (bf16[8192,128]{1,0:T(8,128)(2,1)}, f32[1,256]{1,0:T(1,128)}) custom-call(bf16[8192,128]{1,0:T(8,128)(2,1)} %y_hbm.1, bf16[8192,1024]{1,0:T(8,128)(2,1)} %phi_hbm.1, bf16[256,1024]{1,0:T(8,128)(2,1)} %mix_hbm.1, s32[8,8]{1,0:T(8,128)} %pattern_hbm.1, f32[1,256]{1,0:T(1,128)} %decays_hbm.1, f32[1,256]{1,0:T(1,128)} %bitcast.1), custom_call_target="tpu_custom_call" | custom-call | flops 8589934592 | bytes 20971520 | tf_op jit(solution)/shard_map/pallas_call | solution.py:435
  61.6 0.0 copy-start
  61.6 3.0 %copy.10 = bf16[8192,128]{1,0:T(8,128)(2,1)} copy(bf16[8192,128]{1,0:T(8,128)(2,1)} %get-tuple-element.4) | data formatting | bytes 4194304
  64.7 0.0 copy-done
  64.7 0.6 copy.11
Async XLA Ops:
  61.6 3.1 %copy-start = (f32[1,256]{1,0:T(1,128)S(1)}, f32[1,256]{1,0:T(1,128)}, u32[]{:S(2)}) copy-start(f32[1,256]{1,0:T(1,128)} %get-tuple-element.5) | copy-start | bytes 3076
